TPU v7x, 32 devices: a whole 2x2x4 slice. The times are simulated.
32 devices in a mesh: tok: 8 (over z, x), head: 4 (over y, core).
Axes of the slice: x: 2, y: 2, z: 4, core: 2. Of those that a mesh axis runs over, the one named last changes fastest.
Arguments:
- tokens_in: bfloat16 [12288, 1024], P(('tok', 'head')), may hold values from -6 to 6
- seq_starts: int32 [2], replicated, may hold values from 0 to 11776, as said below
- block_sizes: int32 [2], replicated, may hold values from 128 to 512, as said below
- norm1_gain: float32 [1024], replicated, may hold values from 0.5 to 1.5
- norm1_bias: float32 [1024], replicated, may hold values from -1.75 to 1.75
- w_query: bfloat16 [1024, 1024], replicated, may hold values from -0.1875 to 0.1875
- w_key: bfloat16 [1024, 1024], replicated, may hold values from -0.1875 to 0.1875
- w_value: bfloat16 [1024, 1024], replicated, may hold values from -0.1875 to 0.1875
- w_output: bfloat16 [1024, 1024], replicated, may hold values from -0.75 to 0.75
- ssm_rate: float32 [1024, 16], P('head'), may hold values from 0.2 to 614
- ssm_input: float32 [1024, 16], P('head'), may hold values from -6 to 6
- ssm_output: float32 [1024, 16], P('head'), may hold values from -1.5 to 1.5
- ssm_skip: float32 [1024], P('head'), may hold values from -3 to 3
- norm2_gain: float32 [1024], replicated, may hold values from 0.5 to 1.5
- norm2_bias: float32 [1024], replicated, may hold values from -1.75 to 1.75
- w_up: bfloat16 [1024, 4096], replicated, may hold values from -0.1875 to 0.1875
- up_bias: float32 [4096], replicated, may hold values from -1.75 to 1.75
- w_down: bfloat16 [4096, 1024], replicated, may hold values from -0.09375 to 0.09375
- down_bias: float32 [1024], replicated, may hold values from -1.75 to 1.75
- out_grad: bfloat16 [12288, 1024], P(('tok', 'head')), may hold values from -6 to 6
Outputs:
- layer_out: bfloat16 [12288, 1024], P(('tok', 'head'))
- input_grad: float32 [12288, 1024], P(('tok', 'head'))
- grad_norm1_gain: float32 [1024], P(('tok', 'head'))
- grad_norm1_bias: float32 [1024], P(('tok', 'head'))
- grad_w_query: float32 [1024, 1024], P(('tok', 'head'))
- grad_w_key: float32 [1024, 1024], P(('tok', 'head'))
- grad_w_value: float32 [1024, 1024], P(('tok', 'head'))
- grad_w_output: float32 [1024, 1024], P(('tok', 'head'))
- grad_ssm_rate: float32 [1024, 16], P('head')
- grad_ssm_input: float32 [1024, 16], P('head')
- grad_ssm_output: float32 [1024, 16], P('head')
- grad_ssm_skip: float32 [1024], P('head')
- grad_norm2_gain: float32 [1024], P(('tok', 'head'))
- grad_norm2_bias: float32 [1024], P(('tok', 'head'))
- grad_w_up: float32 [1024, 4096], P(('tok', 'head'))
- grad_up_bias: float32 [4096], P(('tok', 'head'))
- grad_w_down: float32 [4096, 1024], P(('tok', 'head'))
- grad_down_bias: float32 [1024], P(('tok', 'head'))
Inputs may be any that keep to these rules, and one draw needn't show every extreme that they name: seq_starts[0] is 0; the second sequence begins 12288 - L or L positions in, for a length L of 512 to 1535. `block_sizes`: one sequence has blocks of exactly 512 positions.
All inputs are finite; a program needn't handle non-finite values.
Results may differ from a plain program's by a relative error of at most 0.02.
Values may be sent and summed in bfloat16 or wider, within the bound.
A program may use at most 320 MiB of HBM per device.

v0:
```python
import functools
import math

import jax
import jax.numpy as jnp
from jax import lax
from jax.experimental import pallas as pl
from jax.experimental.pallas import tpu as pltpu
from jax.sharding import PartitionSpec as P

epsilon = 1e-05
HD = 128
CTX = 128
BLOCK = 256
NS = 16
SUB = 8
UNROLL = 8
HALF = 8
TILE = 256
MIB = 1 << 20
LOWEST = -1e30
FACTOR = HD ** (-0.5)
FACTOR2 = FACTOR * math.log2(math.e)


def spread(table, n):
    return jnp.broadcast_to(table[n : n + 1, :], (SUB, table.shape[1]))


SCALARS = pl.BlockSpec(memory_space=pltpu.SMEM)


def wide(limit=48):
    return pltpu.CompilerParams(vmem_limit_bytes=limit * MIB)


def across(left, right):
    return lax.dot_general(
        left, right, (((1,), (1,)), ((), ())), preferred_element_type=jnp.float32
    )


def times(left, right):
    return lax.dot_general(
        left, right, (((1,), (0,)), ((), ())), preferred_element_type=jnp.float32
    )


def turn(source, target):
    for at in range(0, source.shape[0], TILE):
        size = min(TILE, source.shape[0] - at)
        piece = source[at : at + size, :].astype(jnp.float32)
        target[:, at : at + size] = piece.T.astype(target.dtype)


def next_block(where_, now):
    second = where_[1]
    length = jnp.where(now >= second, where_[3], where_[2])
    after = now + length
    return jnp.where((now < second) & (after > second), second, after)


REACH = 2 * BLOCK + TILE
BLOCKS = 4


def block_facts(starts, sizes, span):
    anchor = lax.axis_index("tok") * span
    return anchor, starts[1] - anchor, sizes[0], sizes[1]


def block_begin(where_, at):
    opening = jnp.where(at >= where_[1], where_[1], -where_[0])
    length = jnp.where(at >= where_[1], where_[3], where_[2])
    return opening + lax.div(at - opening, length) * length


def block_rows(where_, tile):
    cols = lax.broadcasted_iota(jnp.int32, (1, TILE), 1) + tile * TILE
    begin = block_begin(where_, tile * TILE)
    now, firsts = begin, jnp.zeros_like(cols) + begin
    for _ in range(BLOCKS):
        now = next_block(where_, now)
        firsts = jnp.where(cols >= now, now, firsts)
    return firsts, jnp.where(cols >= where_[1], where_[1], -where_[0]), begin


def joined_rows(rim, own, target):
    target[: rim.shape[0], :] = rim[...]
    target[rim.shape[0] :, :] = own[...]


def local_mask(tile, first):
    rows = lax.broadcasted_iota(jnp.int32, (REACH, TILE), 0) + (tile * TILE - 2 * BLOCK)
    cols = lax.broadcasted_iota(jnp.int32, (1, TILE), 1) + tile * TILE
    return (rows >= first) & (rows <= cols)


def context_at(now):
    return pl.multiple_of((now + 2 * BLOCK) // CTX * CTX, CTX)


def context_mask(start, now, first, opening):
    rows = lax.broadcasted_iota(jnp.int32, (TILE, TILE), 0) + (start - 2 * BLOCK - CTX)
    low = jnp.where(first == now, jnp.maximum(now - CTX, opening), 1 << 28)
    return (rows >= low) & (rows < now)


def lanes_of(head):
    return slice(head * HD, (head + 1) * HD)


def attend_kernel(
    starts,
    sizes,
    query,
    key_own,
    value_own,
    context_own,
    key_rim,
    value_rim,
    context_rim,
    out,
    fine,
    level,
    key,
    value,
    context,
    value_t,
    context_t,
):
    where_ = block_facts(starts, sizes, query.shape[0])
    joined_rows(key_rim, key_own, key)
    joined_rows(value_rim, value_own, value)
    joined_rows(context_rim, context_own, context)
    heads = query.shape[1] // HD
    turn(value, value_t)
    turn(context, context_t)

    def one_tile(tile, _):
        here = pl.ds(pl.multiple_of(tile * TILE, TILE), TILE)
        rows = [query[here, lanes_of(head)] for head in range(heads)]
        firsts, openings, begin = block_rows(where_, tile)

        def score(near, at, head, mask):
            return jnp.where(mask, across(near[at, lanes_of(head)], rows[head]) * FACTOR2, LOWEST)

        def peak(found):
            return jnp.max(found, axis=0, keepdims=True)

        def gather(prob, values_t, at, head):
            low = prob.astype(jnp.bfloat16)
            return (
                jnp.sum(prob, axis=0, keepdims=True),
                jnp.sum(low.astype(jnp.float32), axis=0, keepdims=True),
                times(values_t[lanes_of(head), at], low),
            )

        near_at = pl.ds(pl.multiple_of(tile * TILE, TILE), REACH)
        far_at = pl.ds(context_at(begin), TILE)
        near_mask = local_mask(tile, firsts)
        far_mask = context_mask(context_at(begin), begin, firsts, openings)
        carry = []
        for head in range(heads):
            near = score(key, near_at, head, near_mask)
            far = score(context, far_at, head, far_mask)
            top = jnp.maximum(peak(near), peak(far))
            one = gather(jnp.exp2(near - top), value_t, near_at, head)
            two = gather(jnp.exp2(far - top), context_t, far_at, head)
            carry.append((top,) + tuple(a + b for a, b in zip(one, two)))

        def earlier(state):
            now, carry = state
            start = context_at(now)
            at = pl.ds(start, TILE)
            mask = context_mask(start, now, firsts, openings)
            found = []
            for head in range(heads):
                top, mass, low_mass, total = carry[head]
                far = score(context, at, head, mask)
                new_top = jnp.maximum(top, peak(far))
                shrink = jnp.exp2(top - new_top)
                more = gather(jnp.exp2(far - new_top), context_t, at, head)
                found.append(
                    (new_top,)
                    + tuple(a * shrink + b for a, b in zip((mass, low_mass, total), more))
                )
            return next_block(where_, now), tuple(found)

        _, carry = lax.while_loop(
            lambda state: state[0] < (tile + 1) * TILE,
            earlier,
            (next_block(where_, begin), tuple(carry)),
        )
        for head in range(heads):
            top, mass, low_mass, total = carry[head]
            done = (total / low_mass).T
            fine[here, lanes_of(head)] = done
            out[here, lanes_of(head)] = done.astype(out.dtype)
            level[head, tile] = top + jnp.log2(mass)
        return 0

    lax.fori_loop(0, query.shape[0] // TILE, one_tile, 0)


def attend_back_kernel(
    starts,
    sizes,
    query,
    key_own,
    value_own,
    context_own,
    key_rim,
    value_rim,
    context_rim,
    attended,
    grad,
    level,
    back_query,
    back_key_rim,
    back_value_rim,
    back_context_rim,
    back_key,
    back_value,
    back_context,
    key,
    value,
    context,
    key_t,
    context_t,
    key_sum,
    value_sum,
    context_sum,
):
    where_ = block_facts(starts, sizes, query.shape[0])
    joined_rows(key_rim, key_own, key)
    joined_rows(value_rim, value_own, value)
    joined_rows(context_rim, context_own, context)
    heads = query.shape[1] // HD
    turn(key, key_t)
    turn(context, context_t)
    key_sum[...] = jnp.zeros_like(key_sum)
    value_sum[...] = jnp.zeros_like(value_sum)
    context_sum[...] = jnp.zeros_like(context_sum)

    def one_tile(tile, _):
        here = pl.ds(pl.multiple_of(tile * TILE, TILE), TILE)
        rows = [query[here, lanes_of(head)] for head in range(heads)]
        grads = [grad[here, lanes_of(head)] for head in range(heads)]
        firsts, openings, begin = block_rows(where_, tile)
        levels = [level[head, tile] for head in range(heads)]
        centres = []
        for head in range(heads):
            joint = grads[head].astype(jnp.float32) * attended[here, lanes_of(head)]
            centres.append(jnp.sum(joint.T, axis=0, keepdims=True))

        def slopes(keys, values, at, head, mask):
            found = across(keys[at, lanes_of(head)], rows[head]) * FACTOR2 - levels[head]
            prob = jnp.exp2(jnp.where(mask, found, LOWEST))
            drive = across(values[at, lanes_of(head)], grads[head])
            slope = prob * (drive - centres[head])
            return prob.astype(jnp.bfloat16), slope.astype(jnp.bfloat16)

        def earlier(state):
            now, totals = state
            start = context_at(now)
            at = pl.ds(start, TILE)
            mask = context_mask(start, now, firsts, openings)
            found = []
            for h in range(heads):
                prob, slope = slopes(context, context, at, h, mask)
                context_sum[at, lanes_of(h)] += FACTOR * times(slope, rows[h]) + times(
                    prob, grads[h]
                )
                found.append(totals[h] + times(context_t[lanes_of(h), at], slope))
            return next_block(where_, now), tuple(found)

        at = pl.ds(pl.multiple_of(tile * TILE, TILE), REACH)
        mask = local_mask(tile, firsts)
        totals = []
        for h in range(heads):
            prob, slope = slopes(key, value, at, h, mask)
            key_sum[at, lanes_of(h)] += times(slope, rows[h])
            value_sum[at, lanes_of(h)] += times(prob, grads[h])
            totals.append(times(key_t[lanes_of(h), at], slope))
        state = earlier((begin, tuple(totals)))
        _, totals = lax.while_loop(lambda state: state[0] < (tile + 1) * TILE, earlier, state)
        for head in range(heads):
            back_query[here, lanes_of(head)] = (FACTOR * totals[head]).T.astype(back_query.dtype)
        return 0

    lax.fori_loop(0, query.shape[0] // TILE, one_tile, 0)
    window = 2 * BLOCK
    back_key_rim[...] = (FACTOR * key_sum[:window, :]).astype(back_key_rim.dtype)
    back_value_rim[...] = value_sum[:window, :].astype(back_value_rim.dtype)
    back_context_rim[...] = context_sum[: window + CTX, :].astype(back_context_rim.dtype)
    back_key[...] = FACTOR * key_sum[window:, :]
    back_value[...] = value_sum[window:, :]
    back_context[...] = context_sum[window + CTX :, :]


VMEM = pl.BlockSpec(memory_space=pltpu.VMEM)


def attend(starts, sizes, query, key, value, context, rims):
    rows, width = query.shape
    heads, tiles = width // HD, rows // TILE
    near, far = rows + rims[0].shape[0], rows + rims[2].shape[0]
    low = lambda *shape: pltpu.VMEM(shape, jnp.bfloat16)
    return pl.pallas_call(
        attend_kernel,
        in_specs=[SCALARS] * 2 + [VMEM] * 7,
        out_specs=[VMEM] * 3,
        out_shape=(
            jax.ShapeDtypeStruct((rows, width), jnp.bfloat16),
            jax.ShapeDtypeStruct((rows, width), jnp.float32),
            jax.ShapeDtypeStruct((heads, tiles, 1, TILE), jnp.float32),
        ),
        scratch_shapes=[
            low(near, width),
            low(near, width),
            low(far, width),
            low(width, near),
            low(width, far),
        ],
        compiler_params=wide(60),
        name="attend",
    )(starts, sizes, query, key, value, context, *rims)


def attend_back(starts, sizes, query, key, value, context, rims, attended, grad, level):
    rows, width = query.shape
    near, far = rows + rims[0].shape[0], rows + rims[2].shape[0]
    low = lambda count: jax.ShapeDtypeStruct((count, width), jnp.bfloat16)
    full = lambda count: jax.ShapeDtypeStruct((count, width), jnp.float32)
    lows = lambda *shape: pltpu.VMEM(shape, jnp.bfloat16)
    fulls = lambda *shape: pltpu.VMEM(shape, jnp.float32)
    return pl.pallas_call(
        attend_back_kernel,
        in_specs=[SCALARS] * 2 + [VMEM] * 10,
        out_specs=[VMEM] * 7,
        out_shape=(
            low(rows),
            low(near - rows),
            low(near - rows),
            low(far - rows),
            full(rows),
            full(rows),
            full(rows),
        ),
        scratch_shapes=[
            lows(near, width),
            lows(near, width),
            lows(far, width),
            lows(width, near),
            lows(width, far),
            fulls(near, width),
            fulls(near, width),
            fulls(far, width),
        ],
        compiler_params=wide(60),
        name="attend_back",
    )(starts, sizes, query, key, value, context, *rims, attended, grad, level)


MESH = pl.DeviceIdType.MESH
ROWS = 1024


def bits_of(count):
    return count.bit_length() - 1


def mesh_bits():
    found = []
    tok, head = lax.axis_index("tok"), lax.axis_index("head")
    for axis in ("head", "tok"):
        for level in range(bits_of(lax.axis_size(axis))):
            at = head if axis == "head" else tok
            bit = (at // (1 << level)) % 2
            other = at + (1 - 2 * bit) * (1 << level)
            found.append((bit, (tok, other) if axis == "head" else (other, head)))
    return found


def greet(partners):
    barrier = pltpu.get_barrier_semaphore()
    for partner in partners:
        pl.semaphore_signal(barrier, inc=1, device_id=partner, device_id_type=MESH)
    pl.semaphore_wait(barrier, len(partners))


def halving_orders(bits):
    rest = list(range(4, bits))
    return [
        [0, 1, 2, 3] + rest,
        [0, 2, 1, 3] + rest,
        [0, 3, 2, 1] + rest,
        [0, 3, 1, 2] + rest,
        [0, 2, 3, 1] + rest,
    ]


def slot_of(block, order):
    place = 0
    for bit in order:
        place = place * 2 + (block // (1 << bit)) % 2
    return place


def unpack_refs(function, sizes):
    def kernel(*refs):
        grouped, at = [], 0
        for size in sizes:
            grouped.append(refs[at] if size == 0 else refs[at : at + max(size, 0)])
            at += 1 if size == 0 else max(size, 0)
        function(*grouped)

    return kernel


class Halver:
    def __init__(self, pieces, stages, arrivals, sems, ladder, orders):
        self.now, self.stages, self.arrivals, self.ladder = list(pieces), stages, arrivals, ladder
        self.sems, self.steps = sems, len(ladder)
        self.orders = [halving_orders(self.steps)[order] for order in orders]
        self.sent, self.flying, self.doing = [], {}, {}

    def half(self, stage):
        return 1 << (self.steps - 1 - stage)

    def send(self, number, stage):
        bit, partner = self.ladder[self.orders[number][stage]]
        at = number * len(self.stages) + self.stages.index(stage)
        half = self.half(stage)
        copy = pltpu.make_async_remote_copy(
            src_ref=self.now[number].at[pl.ds((1 - bit) * half, half)],
            dst_ref=self.arrivals[at],
            send_sem=self.sems.at[0, at],
            recv_sem=self.sems.at[1, at],
            device_id=partner,
            device_id_type=MESH,
        )
        copy.start()
        self.sent.append(copy)
        self.flying[number] = (copy, self.arrivals[at], bit * half)
        self.doing[number] = stage

    def absorb(self, number, stage, into=None):
        copy, arrival, keep = self.flying[number]
        copy.wait_recv()
        before = self.now[number]
        target = arrival if into is None else into

        def add(i, _):
            target[i] = before[keep + i] + arrival[i]
            return 0

        lax.fori_loop(0, self.half(stage), add, 0)
        self.now[number] = target

    def part(self, number, stage, keep, leave):
        copy, arrival, base = self.flying[number]
        copy.wait_recv()
        before, half = self.now[number], self.half(stage + 1)
        bit = self.ladder[self.orders[number][stage + 1]][0]
        for at, target in ((bit * half, keep), ((1 - bit) * half, leave)):

            def add(i, _):
                target[i] = before[base + at + i] + arrival[at + i]
                return 0

            lax.fori_loop(0, half, add, 0)

    def last(self, number):
        while self.doing[number] != self.stages[-1]:
            self.advance(number)
        copy, arrival, keep = self.flying[number]
        copy.wait_recv()
        return self.now[number][keep].astype(jnp.float32) + arrival[0].astype(jnp.float32)

    def step(self, stage, into=None):
        for number in range(len(self.now)):
            self.absorb(number, stage, None if into is None else into[number])
            if into is None:
                self.send(number, stage + 1)

    def advance(self, number):
        stage = self.doing[number]
        if stage != self.stages[-1]:
            self.absorb(number, stage)
            self.send(number, stage + 1)

    def begin(self):
        for number in range(len(self.now)):
            self.send(number, self.stages[0])

    def drain(self):
        for copy in self.sent:
            copy.wait_send()


def halver_scratch(pieces, stages, devices):
    steps = bits_of(devices)
    buffers = [
        pltpu.VMEM((1 << (steps - 1 - stage), block, width), jnp.bfloat16)
        for block, width in pieces
        for stage in stages
    ]
    sems = pltpu.SemaphoreType.DMA((2, max(len(buffers), 1)))
    return buffers, len(buffers) or -1, sems


def left_over(pieces, stages, devices):
    slots = 1 << (bits_of(devices) - 1 - stages[-1])
    return [jax.ShapeDtypeStruct((slots, block, width), jnp.bfloat16) for block, width in pieces]


def fill(left, right, start, stop, target, column, order):
    block = target.shape[1]
    each = ROWS // block
    for low in range(start, stop, ROWS):
        high = min(low + ROWS, stop)
        to = column + low - start

        def some_rows(chunk, _):
            at = pl.ds(pl.multiple_of(chunk * ROWS, ROWS), ROWS)
            found = lax.dot_general(
                left[:, at],
                right[:, low:high],
                (((0,), (0,)), ((), ())),
                preferred_element_type=jnp.float32,
            ).astype(jnp.bfloat16)
            for inner in range(each):
                target[slot_of(chunk * each + inner, order), :, to : to + high - low] = found[
                    inner * block : (inner + 1) * block
                ]
            return 0

        lax.fori_loop(0, left.shape[1] // ROWS, some_rows, 0)


def stage_groups(devices):
    steps = bits_of(devices)
    return [0, 1], list(range(2, steps - 1)), [steps - 1]


DOWN_PARTS = (256, 384, 384)
DOWN_ORDERS = (0, 1, 3)
UP_ORDERS = (0, 1, 3)


def swapped(shard, bit):
    heads = bits_of(lax.axis_size("head"))
    axis, level = ("head", bit) if bit < heads else ("tok", bit - heads)
    pairs = [(i, i ^ (1 << level)) for i in range(lax.axis_size(axis))]
    return lax.ppermute(shard, axis, pairs)


UP_PARTS = (((0, 0, 2560),), ((0, 2560, 4096), (1, 0, 256)), ((1, 256, 1024),))
UP_WIDTHS = (2560, 1792, 768)


def products_apart(lefts, rights):
    return [
        lax.psum_scatter(product_left(left, right), ("tok", "head"), scatter_dimension=0, tiled=True)
        for left, right in zip(lefts, rights)
    ]


def tok_peers():
    count, here = lax.axis_size("tok"), lax.axis_index("tok")
    head = lax.axis_index("head")
    return [
        ((lax.rem(here + step, count), head), lax.rem(here + count - step, count))
        for step in range(1, count)
    ]


def share(mine, every, send_sems, recv_sems, place, peers):
    copies = []
    for step, (target, _) in enumerate(peers):
        copy = pltpu.make_async_remote_copy(
            src_ref=mine,
            dst_ref=every.at[place],
            send_sem=send_sems.at[step],
            recv_sem=recv_sems.at[step],
            device_id=target,
            device_id_type=MESH,
        )
        copy.start()
        copies.append(copy)
    return copies


def row_norm(rows, gain, bias):
    rows = rows.astype(jnp.float32)
    centred = rows - jnp.mean(rows, axis=-1, keepdims=True)
    spread_ = jnp.mean(centred * centred, axis=-1, keepdims=True)
    return (centred * lax.rsqrt(spread_ + epsilon) * gain + bias).astype(jnp.bfloat16)


PIECE = 128


def head_backward_kernel(
    stages,
    back_query,
    back_key,
    back_value,
    back_feed,
    hid,
    weights,
    tokens,
    gain,
    grad_middle,
    sums,
    lag_sums,
    skip_sum,
    vectors,
    grad_up_bias,
    up_in,
    input_grad,
    grad_weights,
    row_sum,
    vector_sum,
    up_out,
    total,
    parts,
    near_in,
    far_in,
    products,
    arrived,
    shares,
    head_sems,
    tok_sends,
    tok_recvs,
    share_sends,
    share_recvs,
    every_row,
    row_sends,
    row_recvs,
    vector_parts,
    every_vector,
    tok_sum,
    head_sums,
    vector_sems,
    swap_sems,
    up_arrivals,
    up_sems,
):
    tok, head = lax.axis_index("tok"), lax.axis_index("head")
    heads, toks = lax.axis_size("head"), lax.axis_size("tok")
    near = head + 1 - 2 * lax.rem(head, 2)
    far = head + 2 - 4 * (head // 2)
    across_ = near + 2 - 4 * (near // 2)
    head_peers = [lax.rem(head + step, heads) for step in range(1, heads)]
    ladder = mesh_bits()[bits_of(heads) :]
    peers = tok_peers()
    greet([(tok, other) for other in head_peers] + [target for target, _ in peers])
    rows = input_grad.shape[0]
    states = sums.shape[0]
    every_row[tok] = jnp.zeros_like(every_row[tok])
    every_row[tok, :states] = sums[...]
    every_row[tok, states : 2 * states] = lag_sums[...]
    every_row[tok, 2 * states : 2 * states + 1] = skip_sum[...]
    row_copies = share(every_row.at[tok], every_row, row_sends, row_recvs, tok, peers)
    width = back_query.shape[1]
    columns_ = pl.ds(pl.multiple_of(head * width, HD), width)

    def block_of(owner):
        return pl.ds(pl.multiple_of(owner * rows, PIECE), rows)

    def partial(owner):
        at = block_of(owner)
        found = across(back_query[at, :], weights[:, :width])
        found += across(back_key[at, :], weights[:, width : 2 * width])
        found += across(back_value[at, :], weights[:, 2 * width :])
        total[...] = found
        total[:, columns_] += back_feed[at, :].astype(jnp.float32)

    def copy(source, target, device, number):
        one = pltpu.make_async_remote_copy(
            src_ref=source,
            dst_ref=target,
            send_sem=head_sems.at[0, number],
            recv_sem=head_sems.at[1, number],
            device_id=(tok, device),
            device_id_type=MESH,
        )
        one.start()
        return one

    up_stages = stages[1] + stages[2]
    up = Halver(up_in, up_stages, up_arrivals, up_sems, mesh_bits(), UP_ORDERS)
    up.begin()
    steps = len(ladder)
    orders = [[1, 0] + list(range(2, steps)), list(range(steps))]
    each = products[0].shape[1]
    half_width = products[0].shape[2]
    depth = hid.shape[1]
    base = [0, 0]
    sent = []

    def forward(number, stage):
        bit, partner = ladder[orders[number][stage]]
        half = 1 << (steps - 1 - stage)
        one = pltpu.make_async_remote_copy(
            src_ref=products[number].at[pl.ds(base[number] + (1 - bit) * half, half)],
            dst_ref=arrived[number * steps + stage],
            send_sem=tok_sends.at[number, stage],
            recv_sem=tok_recvs.at[number, stage],
            device_id=partner,
            device_id_type=MESH,
        )
        one.start()
        sent.append(one)
        base[number] = base[number] + bit * half
        return one

    def joined(at, number):
        if number == 0:
            return jnp.concatenate([back_query[at, :], back_key[at, : half_width - width]], axis=1)
        return jnp.concatenate([back_key[at, half_width - width :], back_value[at, :]], axis=1)

    everything = pl.ds(0, hid.shape[0])
    flying = []
    for number in range(2):
        right = joined(everything, number)
        for start in range(0, depth, 512):
            found = lax.dot_general(
                hid[:, start : start + 512],
                right,
                (((0,), (0,)), ((), ())),
                preferred_element_type=jnp.float32,
            ).astype(jnp.bfloat16)
            for inner in range(512 // each):
                products[number][slot_of(start // each + inner, orders[number])] = found[
                    inner * each : (inner + 1) * each
                ]
        flying.append(forward(number, 0))

    partial(across_)
    parts[0] = total[...].astype(jnp.bfloat16)
    first = copy(parts.at[0], near_in.at[0], near, 0)
    partial(near)
    parts[1] = total[...].astype(jnp.bfloat16)
    second = copy(parts.at[1], near_in.at[1], near, 1)
    partial(far)
    first.wait_recv()
    parts[2] = (total[...] + near_in[0].astype(jnp.float32)).astype(jnp.bfloat16)
    third = copy(parts.at[2], far_in, far, 2)
    if up_in:
        up.advance(1)
        up.advance(2)
        up.advance(0)

    partial(head)
    second.wait_recv()
    if up_in:
        up.advance(1)
        up.advance(1)
        up.advance(2)
        up.advance(0)
    total[...] += near_in[1].astype(jnp.float32)

    done = []
    for stage in range(steps):
        for number in range(2):
            flying[number].wait_recv()
            arrival = arrived[number * steps + stage]
            half = 1 << (steps - 1 - stage)
            if stage == steps - 1:
                done.append(
                    products[number][base[number]].astype(jnp.float32)
                    + arrival[0].astype(jnp.float32)
                )
            else:
                for i in range(half):
                    products[number][base[number] + i] = (
                        products[number][base[number] + i] + arrival[i]
                    )
                flying[number] = forward(number, stage + 1)
        if stage == steps - 2:
            third.wait_recv()
            back = total[...] + far_in[...].astype(jnp.float32)
            found = tokens[...].astype(jnp.float32)
            centred = found - jnp.mean(found, axis=-1, keepdims=True)
            scale = lax.rsqrt(jnp.mean(centred * centred, axis=-1, keepdims=True) + epsilon)
            shaped = centred * scale
            lists = [jnp.sum(back * shaped, axis=0, keepdims=True), jnp.sum(back, axis=0, keepdims=True)]
            lists += [vectors[i : i + 1, :] for i in range(3)]
            part = depth // toks
            for place in range(toks):
                for i, row in enumerate(lists):
                    vector_parts[place, i : i + 1, :part] = row[:, place * part : (place + 1) * part]
                for i in range(grad_up_bias.shape[1] // depth):
                    start = place * part * (grad_up_bias.shape[1] // depth) + i * part
                    vector_parts[place, len(lists) + i : len(lists) + i + 1, :part] = grad_up_bias[
                        :, start : start + part
                    ]
            every_vector[tok] = vector_parts[tok]
            vector_copies = []
            for step, (target, _) in enumerate(peers):
                one = pltpu.make_async_remote_copy(
                    src_ref=vector_parts.at[target[0]],
                    dst_ref=every_vector.at[tok],
                    send_sem=vector_sems.at[0, step],
                    recv_sem=vector_sems.at[1, step],
                    device_id=target,
                    device_id_type=MESH,
                )
                one.start()
                vector_copies.append(one)
            back = back * gain[...]
            back = back - jnp.mean(back, axis=-1, keepdims=True)
            back = back - shaped * jnp.mean(back * shaped, axis=-1, keepdims=True)
            input_grad[...] = grad_middle[...] + back * scale
    small = each // heads
    ready, landed = shares
    for other in range(heads):
        for number in range(2):
            ready[other, :, number * half_width : (number + 1) * half_width] = done[number][
                other * small : (other + 1) * small
            ].astype(ready.dtype)
    landed[head] = ready[head]
    swaps = []
    for step, other in enumerate(head_peers):
        one = pltpu.make_async_remote_copy(
            src_ref=ready.at[other],
            dst_ref=landed.at[head],
            send_sem=share_sends.at[step],
            recv_sem=share_recvs.at[step],
            device_id=(tok, other),
            device_id_type=MESH,
        )
        one.start()
        swaps.append(one)

    for one in row_copies + vector_copies:
        one.wait_recv()
    row_sum[...] = jnp.sum(every_row[...], axis=0)
    tok_sum[...] = jnp.sum(every_vector[...], axis=0)
    head_sums[head] = tok_sum[...]
    head_copies = []
    for step, other in enumerate(head_peers):
        one = pltpu.make_async_remote_copy(
            src_ref=tok_sum,
            dst_ref=head_sums.at[head],
            send_sem=swap_sems.at[0, step],
            recv_sem=swap_sems.at[1, step],
            device_id=(tok, other),
            device_id_type=MESH,
        )
        one.start()
        head_copies.append(one)
    for one in swaps:
        one.wait()
    for other in range(heads):
        for kind in range(3):
            grad_weights[kind][:, other * width : (other + 1) * width] = landed[
                other, :, kind * width : (kind + 1) * width
            ].astype(jnp.float32)
    for one in head_copies:
        one.wait_recv()
    vector_sum[...] = jnp.sum(head_sums[...], axis=0)
    for number in range(len(up_in)):
        found, column = up.last(number), 0
        for pair, start, stop in UP_PARTS[number]:
            up_out[pair][:, start:stop] = found[:, column : column + stop - start]
            column += stop - start
    up.drain()
    for one in sent + [first, second, third] + row_copies + vector_copies + head_copies:
        one.wait_send()


def head_backward(
    back_query,
    back_key,
    back_value,
    back_feed,
    hid,
    weights,
    tokens,
    gain,
    grad_middle,
    sums,
    lag_sums,
    skip_sum,
    vectors,
    grad_up_bias,
    up,
    collective_id,
):
    span, width = back_query.shape
    depth = hid.shape[1]
    heads, toks = lax.axis_size("head"), lax.axis_size("tok")
    rows, each = span // heads, depth // toks
    steps, half_width = bits_of(toks), 3 * width // 2
    swap_kind = jnp.bfloat16 if each // heads % 16 == 0 else jnp.float32
    devices = heads * toks
    stages = stage_groups(devices)
    up_pieces = [piece.shape[1:] for piece in up]
    up_buffers, up_count, up_sems = halver_scratch(up_pieces, stages[1] + stages[2], devices)
    outs = []
    for pair in range(2 if up else 0):
        stop = max(part[2] for parts in UP_PARTS for part in parts if part[0] == pair)
        outs.append(jax.ShapeDtypeStruct((up_pieces[0][0], stop), jnp.float32))
    states = sums.shape[0]
    states += -states % SUB
    row_count = 2 * states + SUB
    part = (16, max(depth // toks, HD))
    ups = len(up) or -1
    low = lambda *shape: pltpu.VMEM(shape, jnp.bfloat16)
    full = lambda *shape: pltpu.VMEM(shape, jnp.float32)
    sems = lambda *shape: pltpu.SemaphoreType.DMA(shape)
    sizes = [0] * 14 + [ups, 0, 3, 0, 0, len(outs) or -1] + [0] * 4 + [2, 2 * steps, 2]
    sizes += [0] * 5 + [0] * 9 + [up_count, 0]
    found = pl.pallas_call(
        unpack_refs(functools.partial(head_backward_kernel, stages), sizes),
        in_specs=[VMEM] * (14 + len(up)),
        out_specs=[VMEM] * (6 + len(outs)),
        out_shape=[
            jax.ShapeDtypeStruct((rows, depth), jnp.float32),
        ]
        + [jax.ShapeDtypeStruct((each // heads, depth), jnp.float32)] * 3
        + [
            jax.ShapeDtypeStruct((row_count, width), jnp.float32),
            jax.ShapeDtypeStruct(part, jnp.float32),
        ]
        + outs,
        scratch_shapes=[
            full(rows, depth),
            low(3, rows, depth),
            low(2, rows, depth),
            low(rows, depth),
        ]
        + [low(toks, each, half_width)] * 2
        + [low(1 << (steps - 1 - stage), each, half_width) for stage in range(steps)] * 2
        + [pltpu.VMEM((heads, each // heads, 3 * width), swap_kind)] * 2
        + [sems(2, 3), sems(2, steps), sems(2, steps), sems(heads - 1), sems(heads - 1)]
        + [full(toks, row_count, width), sems(toks - 1), sems(toks - 1)]
        + [full(toks, *part), full(toks, *part), full(*part), full(heads, *part)]
        + [sems(2, toks - 1), sems(2, heads - 1)]
        + up_buffers
        + [up_sems],
        compiler_params=pltpu.CompilerParams(
            collective_id=collective_id, has_side_effects=True, vmem_limit_bytes=58 * MIB
        ),
        name="head_backward",
    )(
        back_query,
        back_key,
        back_value,
        back_feed,
        hid,
        weights,
        tokens,
        gain,
        grad_middle,
        sums,
        lag_sums,
        skip_sum,
        vectors,
        grad_up_bias,
        *up,
    )
    return found[0], found[1:4], found[4], found[5], found[6:]


def every_step(length, second, back, body, carry):
    begins = lax.broadcasted_iota(jnp.int32, (SUB, HD), 0) * length - second

    def some(block, now):
        for inner in range(UNROLL):
            t = block * UNROLL + inner
            at = length - 1 - t if back else t
            now = body(at, now, jnp.where(begins == -at, 0.0, 1.0))
        return now

    return lax.fori_loop(0, length // UNROLL, some, carry)


def kept(second, begin, end):
    return jnp.where((second >= begin) & (second < end), 0.0, 1.0)


def decay_tables(rate, span):
    length = span // SUB
    return (
        jnp.exp(-rate),
        jnp.exp(-rate * length),
        length * jnp.exp(-rate * (length - 1)),
        jnp.exp(-rate * span),
        span * jnp.exp(-rate * (span - 1)),
    )


def front_kernel(
    seq_starts,
    tokens,
    gain,
    bias,
    rate,
    mix,
    skip,
    w_query,
    w_key,
    w_value,
    hid,
    query,
    key,
    value,
    feed_rows,
    weights,
    context,
    key_rim,
    value_rim,
    context_rim,
    gathered,
    drives,
    total,
    ends,
    mine,
    every,
    send_sems,
    recv_sems,
    load_sems,
    share_sends,
    share_recvs,
    rim_sems,
):
    tok, head = lax.axis_index("tok"), lax.axis_index("head")
    near = head + 1 - 2 * lax.rem(head, 2)
    far = head + 2 - 4 * (head // 2)
    across_ = near + 2 - 4 * (near // 2)
    peers = tok_peers()
    greet([(tok, near), (tok, far)] + [target for target, _ in peers])
    rows = tokens.shape[0]
    pieces = rows // PIECE
    width = query.shape[1]
    columns_ = pl.ds(pl.multiple_of(head * width, HD), width)
    loads = [
        pltpu.make_async_copy(
            whole.at[:, columns_], weights.at[:, pl.ds(kind * width, width)], load_sems.at[kind]
        )
        for kind, whole in enumerate((w_query, w_key, w_value))
    ]
    for load in loads:
        load.start()

    def copy(source, owner, target, number):
        return pltpu.make_async_remote_copy(
            src_ref=source,
            dst_ref=gathered.at[owner, pl.ds(number % pieces * PIECE, PIECE)],
            send_sem=send_sems.at[number],
            recv_sem=recv_sems.at[number],
            device_id=(tok, target),
            device_id_type=MESH,
        )

    def own(number):
        return tokens.at[pl.ds(number * PIECE, PIECE)]

    afar = [copy(own(i), head, far, i) for i in range(pieces)]
    beside = [copy(own(i), head, near, pieces + i) for i in range(pieces)]
    for one in afar + beside:
        one.start()

    def work(found, owner, number):
        at = pl.ds(pl.multiple_of(owner * rows + number * PIECE, PIECE), PIECE)
        low = row_norm(found, gain[...], bias[...])
        hid[at, :] = low
        feed_rows[at, :] = hid[at, columns_]
        mixed = jnp.dot(low, weights[...], preferred_element_type=jnp.float32).astype(
            jnp.bfloat16
        )
        query[at, :] = mixed[:, :width]
        key[at, :] = mixed[:, width : 2 * width]
        value[at, :] = mixed[:, 2 * width :]

    def block(owner, number):
        return gathered[owner, number * PIECE : (number + 1) * PIECE, :]

    for load in loads:
        load.wait()
    for i in range(pieces):
        work(tokens[i * PIECE : (i + 1) * PIECE, :], head, i)
    for i in range(pieces):
        beside[i].wait_recv()
        work(block(near, i), near, i)
    passed = []
    for i in range(pieces):
        afar[i].wait_recv()
        one = copy(
            gathered.at[far, pl.ds(i * PIECE, PIECE)], far, near, 2 * pieces + i
        )
        one.start()
        passed.append(one)
        work(block(far, i), far, i)
    for i in range(pieces):
        passed[i].wait_recv()
        work(block(across_, i), across_, i)

    here, count = tok, every.shape[0]
    decay, chunk_decay, _, span_decay, _ = decay_tables(rate[...], feed_rows.shape[0])
    length = feed_rows.shape[0] // SUB
    span = feed_rows.shape[0]
    second = seq_starts[1] - here * span
    keep = [kept(second, chunk * length, (chunk + 1) * length) for chunk in range(SUB)]
    groups = feed_rows.shape[1] // HD
    zero = jnp.zeros((SUB, HD), jnp.float32)

    def rim(source, target, number):
        copy = pltpu.make_async_remote_copy(
            src_ref=source,
            dst_ref=target,
            send_sem=rim_sems.at[0, number],
            recv_sem=rim_sems.at[1, number],
            device_id=peers[0][0],
            device_id_type=MESH,
        )

        @pl.when(here < count - 1)
        def _():
            copy.start()

        return copy

    @pl.when(here == 0)
    def _():
        for target in (key_rim, value_rim, context_rim):
            target[...] = jnp.zeros_like(target)

    window = key_rim.shape[0]
    sent = [rim(key.at[pl.ds(span - window, window)], key_rim, 0)]
    for group in range(groups):
        lanes = slice(group * HD, (group + 1) * HD)
        drives[group] = feed_rows[:, lanes].astype(jnp.float32)
        factors = [spread(decay[:, lanes], n) for n in range(NS)]

        def end_step(t, states, live):
            drive = drives[group, pl.ds(t, SUB, stride=length), :]
            return tuple(s * live * f + drive for s, f in zip(states, factors))

        done = every_step(length, second, False, end_step, (zero,) * NS)
        for n in range(NS):
            ends[n, :, lanes] = done[n]
    now = ends[:, 0, :]
    for chunk in range(1, SUB):
        now = keep[chunk] * (chunk_decay * now) + ends[:, chunk, :]
    mine[...] = now
    every[here] = now
    copies = share(mine, every, share_sends, share_recvs, here, peers)
    sent.append(rim(value.at[pl.ds(span - window, window)], value_rim, 1))
    for copy in copies:
        copy.wait()
    now = jnp.zeros_like(span_decay)
    for place in range(count - 1):
        whole = kept(seq_starts[1], place * span, (place + 1) * span)
        now = jnp.where(place < here, whole * (span_decay * now) + every[place], now)
    for chunk in range(SUB):
        own = ends[:, chunk, :]
        ends[:, chunk, :] = now
        now = keep[chunk] * (chunk_decay * now) + own

    window = context_rim.shape[0]
    for group in range(groups):
        lanes = slice(group * HD, (group + 1) * HD)
        factors = [spread(decay[:, lanes], n) for n in range(NS)]
        mixes = [spread(mix[:, lanes], n) for n in range(NS)]
        direct = spread(skip[:, lanes], 0)

        def out_step(t, states, live):
            at = pl.ds(t, SUB, stride=length)
            drive = drives[group, at, :]
            states = tuple(s * live * f + drive for s, f in zip(states, factors))
            parts = [state * weight for state, weight in zip(states, mixes)] + [direct * drive]
            while len(parts) > 1:
                parts = [a + b for a, b in zip(parts[::2], parts[1::2])] + (
                    [parts[-1]] if len(parts) % 2 else []
                )
            total[group, at, :] = parts[0]
            return states

        every_step(
            length, second, False, out_step, tuple(ends[n, :, lanes] for n in range(NS))
        )
        context[:, lanes] = total[group].astype(context.dtype)
        sent.append(
            rim(
                context.at[pl.ds(span - window, window), pl.ds(group * HD, HD)],
                context_rim.at[:, pl.ds(group * HD, HD)],
                2 + group,
            )
        )
    @pl.when(here > 0)
    def _():
        for copy in sent:
            copy.wait_recv()

    @pl.when(here < count - 1)
    def _():
        for copy in sent:
            copy.wait_send()

    for one in afar + beside + passed:
        one.wait_send()


def front(seq_starts, tokens, gain, bias, rate, mix, skip, w_query, w_key, w_value, collective_id):
    rows, depth = tokens.shape
    heads, toks = lax.axis_size("head"), lax.axis_size("tok")
    span, width = rows * heads, w_query.shape[1] // heads
    groups, window = width // HD, 2 * BLOCK
    low = lambda count: jax.ShapeDtypeStruct((span, count), jnp.bfloat16)
    rim = lambda count: jax.ShapeDtypeStruct((count, width), jnp.bfloat16)
    fulls = lambda *shape: pltpu.VMEM(shape, jnp.float32)
    sems = lambda *shape: pltpu.SemaphoreType.DMA(shape)
    found = pl.pallas_call(
        front_kernel,
        in_specs=[SCALARS] + [VMEM] * 6 + [pl.BlockSpec(memory_space=pl.ANY)] * 3,
        out_specs=[VMEM] * 10,
        out_shape=[
            low(depth),
            low(width),
            low(width),
            low(width),
            low(width),
            jax.ShapeDtypeStruct((depth, 3 * width), jnp.bfloat16),
            low(width),
            rim(window),
            rim(window),
            rim(window + CTX),
        ],
        scratch_shapes=[
            pltpu.VMEM((heads, rows, depth), jnp.bfloat16),
            fulls(groups, span, HD),
            fulls(groups, span, HD),
            fulls(NS, SUB, width),
            fulls(NS, width),
            fulls(toks, NS, width),
            sems(3 * (rows // PIECE)),
            sems(3 * (rows // PIECE)),
            sems(3),
            sems(toks - 1),
            sems(toks - 1),
            sems(2, 2 + groups),
        ],
        compiler_params=pltpu.CompilerParams(
            collective_id=collective_id, has_side_effects=True, vmem_limit_bytes=60 * MIB
        ),
        name="front",
    )(seq_starts, tokens, gain, bias, rate, mix, skip, w_query, w_key, w_value)
    return tuple(found[:7]) + (found[7:],)


def recurrence_back_kernel(
    stages,
    seq_starts,
    slope,
    feed_rows,
    rate,
    mix,
    skip,
    key_sum,
    value_sum,
    key_rim,
    value_rim,
    context_rim,
    lefts,
    rights,
    down_keep,
    down_come,
    back_key,
    back_value,
    back,
    sums,
    lag_sums,
    skip_sum,
    down_out,
    up_out,
    slopes,
    rows,
    total,
    ends,
    lags,
    mine,
    every,
    share_sends,
    share_recvs,
    key_in,
    value_in,
    context_in,
    rim_sems,
    down_now,
    down_arrivals,
    down_sems,
    grads,
    up_arrivals,
    up_sems,
):
    here, count = lax.axis_index("tok"), every.shape[0]
    peers = tok_peers()
    ladder = mesh_bits()
    heads = bits_of(lax.axis_size("head"))
    greet([target for target, _ in peers] + [partner for _, partner in ladder[:heads]])

    rims = []
    for number, (source, target) in enumerate(
        ((context_rim, context_in), (key_rim, key_in), (value_rim, value_in))
    ):
        rims.append(
            pltpu.make_async_remote_copy(
                src_ref=source,
                dst_ref=target,
                send_sem=rim_sems.at[0, number],
                recv_sem=rim_sems.at[1, number],
                device_id=peers[-1][0],
                device_id_type=MESH,
            )
        )

    @pl.when(here == count - 1)
    def _():
        for target in (context_in, key_in, value_in):
            target[...] = jnp.zeros_like(target)

    @pl.when(here > 0)
    def _():
        for copy in rims:
            copy.start()

    down_stages = stages[1] + stages[2]
    down = Halver(down_now, down_stages, down_arrivals, down_sems, ladder, DOWN_ORDERS)
    for number in (1, 2, 0):
        down_now[number][...] = down_keep[number][...] + down_come[number][...]
        if number:
            down.send(number, down_stages[0])
    up = Halver(grads, stages[0], up_arrivals, up_sems, ladder, UP_ORDERS)
    for number, parts in enumerate(UP_PARTS if grads else ()):
        column = 0
        for pair, start, stop in parts:
            fill(
                lefts[pair], rights[pair], start, stop, grads[number], column, up.orders[number]
            )
            column += stop - start
        up.send(number, stages[0][0])
    if grads:
        up.absorb(0, stages[0][0])
        up.send(0, stages[0][1])

    @pl.when(here < count - 1)
    def _():
        rims[0].wait_recv()

    span = slope.shape[0]
    decay, factor, bend, over, over_slope = decay_tables(rate[...], span)
    length = span // SUB
    second = seq_starts[1] - here * span
    keep = [kept(second, chunk * length, (chunk + 1) * length) for chunk in range(SUB)]
    groups = slope.shape[1] // HD
    zero = jnp.zeros((SUB, HD), jnp.float32)
    for group in range(groups):
        lanes = slice(group * HD, (group + 1) * HD)
        slopes[group] = slope[:, lanes]
        slopes[group, span - context_in.shape[0] :, :] += context_in[:, lanes].astype(jnp.float32)
        rows[group] = feed_rows[:, lanes].astype(jnp.float32)
        total[group] = slopes[group] * skip[:, lanes]
        skip_sum[:, lanes] = jnp.sum(slopes[group] * rows[group], axis=0, keepdims=True)
        factors = [spread(decay[:, lanes], n) for n in range(NS)]

        def end_step(t, carry, live):
            drive = slopes[group, pl.ds(t, SUB, stride=length), :]
            adjoint, lag = carry[:NS], carry[NS:]
            lag = [(a * f + b) * live for a, f, b in zip(lag, factors, adjoint)]
            adjoint = [(a * f + drive) * live for a, f in zip(adjoint, factors)]
            return tuple(adjoint) + tuple(lag)

        done = every_step(length, second, True, end_step, (zero,) * (2 * NS))
        for n in range(NS):
            ends[n, :, lanes] = done[n]
            lags[n, :, lanes] = done[NS + n]

    now, late = ends[:, SUB - 1, :], lags[:, SUB - 1, :]
    for chunk in reversed(range(SUB - 1)):
        late = keep[chunk] * (factor * late + bend * now) + lags[:, chunk, :]
        now = keep[chunk] * (factor * now) + ends[:, chunk, :]
    mine[0] = now
    mine[1] = late
    every[here, 0] = now
    every[here, 1] = late
    copies = share(mine, every, share_sends, share_recvs, here, peers)

    down.send(0, down_stages[0])
    down.advance(1)
    down.advance(2)
    for number in range(1, len(grads)):
        up.absorb(number, stages[0][0])
        up.send(number, stages[0][1])
    for copy in copies:
        copy.wait()
    now, late = jnp.zeros_like(over), jnp.zeros_like(over)
    for place in reversed(range(1, count)):
        reached = place > here
        whole = kept(seq_starts[1], place * span, (place + 1) * span)
        late = jnp.where(reached, whole * (over * late + over_slope * now) + every[place, 1], late)
        now = jnp.where(reached, whole * (over * now) + every[place, 0], now)
    for chunk in reversed(range(SUB)):
        own, own_late = ends[:, chunk, :], lags[:, chunk, :]
        ends[:, chunk, :] = now
        lags[:, chunk, :] = late
        late = keep[chunk] * (factor * late + bend * now) + own_late
        now = keep[chunk] * (factor * now) + own

    for group in range(groups):
        lanes = slice(group * HD, (group + 1) * HD)
        for base in range(0, NS, HALF):
            factors = [spread(decay[:, lanes], base + n) for n in range(HALF)]
            mixes = [spread(mix[:, lanes], base + n) for n in range(HALF)]

            def out_step(t, carry, live):
                at = pl.ds(t, SUB, stride=length)
                drive, source = slopes[group, at, :], rows[group, at, :]
                adjoint, lag = carry[:HALF], carry[HALF : 2 * HALF]
                direct, late_sum = carry[2 * HALF : 3 * HALF], carry[3 * HALF :]
                lag = [a * f + b for a, f, b in zip(lag, factors, adjoint)]
                adjoint = [a * f + drive for a, f in zip(adjoint, factors)]
                direct = [a + b * source for a, b in zip(direct, adjoint)]
                late_sum = [a + b * source for a, b in zip(late_sum, lag)]
                parts = [a * b for a, b in zip(adjoint, mixes)]
                while len(parts) > 1:
                    parts = [a + b for a, b in zip(parts[::2], parts[1::2])]
                total[group, at, :] = total[group, at, :] + parts[0]
                lag = [a * live for a in lag]
                adjoint = [a * live for a in adjoint]
                return tuple(adjoint) + tuple(lag) + tuple(direct) + tuple(late_sum)

            if group == 0 and base > 0:
                down.advance(0)
                down.advance(1)
                down.advance(2)
            if group == 1 and base == 0:
                down.advance(0)
            first = tuple(ends[base + n, :, lanes] for n in range(HALF)) + tuple(
                lags[base + n, :, lanes] for n in range(HALF)
            )
            done = every_step(length, second, True, out_step, first + (zero,) * (2 * HALF))
            for n in range(HALF):
                sums[base + n : base + n + 1, lanes] = jnp.sum(
                    done[2 * HALF + n], axis=0, keepdims=True
                )
                lag_sums[base + n : base + n + 1, lanes] = jnp.sum(
                    done[3 * HALF + n], axis=0, keepdims=True
                )
        back[:, lanes] = total[group].astype(back.dtype)
    finished = [down.last(number) for number in range(len(down_now))]
    column = 0
    for piece in finished:
        down_out[:, column : column + piece.shape[1]] = piece
        column += piece.shape[1]

    @pl.when(here < count - 1)
    def _():
        rims[1].wait_recv()
        rims[2].wait_recv()

    inner = span - key_in.shape[0]
    for source, more, target in (
        (key_sum, key_in, back_key),
        (value_sum, value_in, back_value),
    ):
        target[:inner, :] = source[:inner, :].astype(target.dtype)
        target[inner:, :] = (source[inner:, :] + more[...].astype(jnp.float32)).astype(
            target.dtype
        )
    up.step(stages[0][1], up_out)
    down.drain()
    up.drain()

    @pl.when(here > 0)
    def _():
        for copy in rims:
            copy.wait_send()


def recurrence_back(
    seq_starts, slope, feed_rows, rate, mix, skip, sums, rims, lefts, rights, down, collective_id
):
    span, width = feed_rows.shape
    toks = lax.axis_size("tok")
    devices = toks * lax.axis_size("head")
    stages = stage_groups(devices)
    block = lefts[0].shape[1] // devices
    apart, up_pieces = None, [(block, part) for part in UP_WIDTHS]
    if block < 16:
        apart = products_apart(lefts, rights)
        lefts, rights, up_pieces = [], [], []
    keep, come = down
    down_pieces = [piece.shape[1:] for piece in keep]
    late = stages[1] + stages[2]
    down_buffers, down_count, down_sems = halver_scratch(down_pieces, late, devices)
    up_buffers, up_count, up_sems = halver_scratch(up_pieces, stages[0], devices)
    down_width = sum(piece[1] for piece in down_pieces)
    up_shapes = left_over(up_pieces, stages[0], devices)
    full = lambda *shape: jax.ShapeDtypeStruct(shape, jnp.float32)
    fulls = lambda *shape: pltpu.VMEM(shape, jnp.float32)
    sems = lambda *shape: pltpu.SemaphoreType.DMA(shape)
    groups = width // HD
    scratch = [
        fulls(groups, span, HD),
        fulls(groups, span, HD),
        fulls(groups, span, HD),
        fulls(NS, SUB, width),
        fulls(NS, SUB, width),
        fulls(2, NS, width),
        fulls(toks, 2, NS, width),
        sems(toks - 1),
        sems(toks - 1),
    ]
    low = lambda count: jax.ShapeDtypeStruct((count, width), jnp.bfloat16)
    scratch += [pltpu.VMEM(rims[k].shape, jnp.bfloat16) for k in (0, 1, 2)]
    scratch += [sems(2, 3)] + [pltpu.VMEM(piece.shape, jnp.bfloat16) for piece in keep]
    scratch += down_buffers + [down_sems]
    scratch += [pltpu.VMEM((devices,) + piece, jnp.bfloat16) for piece in up_pieces]
    scratch += up_buffers + [up_sems]
    pairs, ups, downs = len(lefts) or -1, len(up_pieces) or -1, len(keep)
    sizes = [0] * 11 + [pairs, pairs, downs, downs] + [0] * 6 + [0, ups] + [0] * 9
    sizes += [0] * 4 + [downs, down_count, 0, ups, up_count, 0]
    found = pl.pallas_call(
        unpack_refs(functools.partial(recurrence_back_kernel, stages), sizes),
        in_specs=[SCALARS] + [VMEM] * (10 + 2 * len(lefts) + 2 * downs),
        out_specs=[VMEM] * (7 + len(up_shapes)),
        out_shape=[
            low(span),
            low(span),
            low(span),
            full(NS, width),
            full(NS, width),
            full(1, width),
        ]
        + [full(down_pieces[0][0], down_width)]
        + up_shapes,
        scratch_shapes=scratch,
        compiler_params=pltpu.CompilerParams(
            collective_id=collective_id, has_side_effects=True, vmem_limit_bytes=60 * MIB
        ),
        name="recurrence_back",
    )(
        seq_starts,
        slope,
        feed_rows,
        rate,
        mix,
        skip,
        *sums,
        *rims,
        *lefts,
        *rights,
        *keep,
        *come,
    )
    return tuple(found[:6]) + (found[6], found[7:], apart)


CHUNK = 1024
UP_CHUNK = 512
ROOT = math.sqrt(2.0 / math.pi)
CUBIC = 0.044715


def feed_kernel(
    stages,
    attended,
    tokens,
    out_grad,
    gain,
    bias,
    up_bias,
    down_bias,
    w_output,
    w_up,
    w_down,
    layer_out,
    grad_middle,
    normed,
    grad_before,
    joined,
    grad_branch,
    grad_att,
    down_left,
    vectors,
    grad_up_bias,
    output_w,
    up_w,
    down_w,
    split,
    active,
    bend,
    drive,
    shape,
    down_sum,
    back_sum,
    grad_split,
    grads,
    arrivals,
    weight_sems,
    down_sems,
    head_sems,
    halver_sems,
):
    tok, head = lax.axis_index("tok"), lax.axis_index("head")
    heads = lax.axis_size("head")
    rows, width = tokens.shape[0], attended.shape[1]
    hidden = up_w.shape[1]
    loads = [
        pltpu.make_async_copy(source, target, weight_sems.at[number])
        for number, (source, target) in enumerate(
            ((w_output, output_w), (w_up, up_w))
        )
    ]

    def down_load(chunk):
        slot = lax.rem(chunk, 2)
        return pltpu.make_async_copy(
            w_down.at[pl.ds(pl.multiple_of(chunk * CHUNK, CHUNK), CHUNK)],
            down_w.at[slot],
            down_sems.at[slot],
        )

    for load in loads:
        load.start()
    for chunk in range(2):
        down_load(chunk).start()
    peers = [lax.rem(head + step, heads) for step in range(1, heads)]
    ladder = mesh_bits()
    greet([(tok, other) for other in peers] + [p for _, p in ladder[bits_of(heads) :]])

    def block_of(owner):
        return pl.ds(pl.multiple_of(owner * rows, PIECE), rows)

    def swap(source_of, target, kind):
        found = []
        for step, other in enumerate(peers):
            copy = pltpu.make_async_remote_copy(
                src_ref=source_of(other),
                dst_ref=target,
                send_sem=head_sems.at[kind, 0, step],
                recv_sem=head_sems.at[kind, 1, step],
                device_id=(tok, other),
                device_id_type=MESH,
            )
            copy.start()
            found.append(copy)
        return found

    def drive_chunk(chunk, _):
        at = pl.ds(pl.multiple_of(chunk * CHUNK, CHUNK), CHUNK)
        down_load(chunk).wait()
        drive[:, at] = across(out_grad[...], down_w[lax.rem(chunk, 2)]).astype(jnp.bfloat16)
        down_load(lax.rem(chunk + 2, chunks)).start()
        return 0

    chunks = hidden // CHUNK
    first = swap(lambda other: attended.at[block_of(other)], split.at[head], 0)
    split[head] = attended[block_of(head), :]
    lax.fori_loop(0, chunks, drive_chunk, 0)
    loads[0].wait()
    for copy in first:
        copy.wait_recv()
    total = tokens[...].astype(jnp.float32)
    for owner in range(heads):
        at = slice(owner * width, (owner + 1) * width)
        joined[:, at] = split[owner]
        total += jnp.dot(split[owner], output_w[at, :], preferred_element_type=jnp.float32)
    grad_middle[...] = total
    centred = total - jnp.mean(total, axis=-1, keepdims=True)
    scale = lax.rsqrt(jnp.mean(centred * centred, axis=-1, keepdims=True) + epsilon)
    shape[...] = centred * scale
    normed[...] = (centred * scale * gain[...] + bias[...]).astype(jnp.bfloat16)

    loads[1].wait()

    def up_chunk(chunk, _):
        at = pl.ds(pl.multiple_of(chunk * UP_CHUNK, UP_CHUNK), UP_CHUNK)
        before = jnp.dot(normed[...], up_w[:, at], preferred_element_type=jnp.float32)
        before += up_bias[:, at]
        square = before * before
        bent = jnp.tanh(ROOT * before * (1.0 + CUBIC * square))
        half = 0.5 * (1.0 + bent)
        active[:, at] = (before * half).astype(jnp.bfloat16)
        bend[:, at] = half + (0.5 * ROOT) * before * (1.0 - bent * bent) * (
            1.0 + (3.0 * CUBIC) * square
        )
        return 0

    lax.fori_loop(0, hidden // UP_CHUNK, up_chunk, 0)
    halver = Halver(grads, stages, arrivals, halver_sems, ladder, DOWN_ORDERS)
    starts = [sum(DOWN_PARTS[:k]) for k in range(len(DOWN_PARTS) + 1)]
    for k, order in enumerate(halver.orders):
        fill(active, out_grad, starts[k], starts[k + 1], grads[k], 0, order)
        halver.send(k, stages[0])

    back_sum[...] = jnp.zeros_like(back_sum)

    def back_chunk(chunk, _):
        at = pl.ds(pl.multiple_of(chunk * CHUNK, CHUNK), CHUNK)
        low = (drive[:, at].astype(jnp.float32) * bend[:, at]).astype(jnp.bfloat16)
        grad_before[:, at] = low
        grad_up_bias[:, at] = jnp.sum(low.astype(jnp.float32), axis=0, keepdims=True)
        back_sum[...] += across(low, up_w[:, at])
        return 0

    lax.fori_loop(0, chunks, back_chunk, 0)
    back = back_sum[...]
    shaped = shape[...]
    vectors[0:1, :] = jnp.sum(back * shaped, axis=0, keepdims=True)
    vectors[1:2, :] = jnp.sum(back, axis=0, keepdims=True)
    top = out_grad[...].astype(jnp.float32)
    vectors[2:3, :] = jnp.sum(top, axis=0, keepdims=True)
    back = back * gain[...]
    back = back - jnp.mean(back, axis=-1, keepdims=True)
    back = back - shaped * jnp.mean(back * shaped, axis=-1, keepdims=True)
    total = grad_middle[...]
    centred = total - jnp.mean(total, axis=-1, keepdims=True)
    scale = lax.rsqrt(jnp.mean(centred * centred, axis=-1, keepdims=True) + epsilon)
    down_sum[...] = total + down_bias[...]
    top = top + back * scale
    grad_middle[...] = top
    low = top.astype(jnp.bfloat16)
    grad_branch[...] = low
    for owner in range(heads):
        at = slice(owner * width, (owner + 1) * width)
        grad_split[owner] = across(low, output_w[at, :]).astype(jnp.bfloat16)
    second = swap(lambda other: grad_split.at[other], grad_att.at[block_of(head)], 1)
    grad_att[block_of(head), :] = grad_split[head]

    def down_chunk(chunk, _):
        at = pl.ds(pl.multiple_of(chunk * CHUNK, CHUNK), CHUNK)
        down_load(chunk).wait()
        down_sum[...] += jnp.dot(
            active[:, at], down_w[lax.rem(chunk, 2)], preferred_element_type=jnp.float32
        )

        @pl.when(chunk + 2 < chunks)
        def _():
            down_load(chunk + 2).start()

        return 0

    for k in range(len(grads)):
        halver.part(k, stages[0], down_left[2 * k], down_left[2 * k + 1])
    lax.fori_loop(0, chunks, down_chunk, 0)
    layer_out[...] = down_sum[...].astype(jnp.bfloat16)
    for copy in second:
        copy.wait_recv()
    halver.drain()
    for copy in first + second:
        copy.wait_send()


def feed(
    attended,
    tokens,
    out_grad,
    gain,
    bias,
    up_bias,
    down_bias,
    w_output,
    w_up,
    w_down,
    collective_id,
):
    rows, depth = tokens.shape
    span, width = attended.shape
    hidden = w_up.shape[1]
    heads = lax.axis_size("head")
    devices = heads * lax.axis_size("tok")
    block = hidden // devices
    stages = stage_groups(devices)[0][:1]
    pieces = [(block, part) for part in DOWN_PARTS]
    buffers, buffer_count, halver_sems = halver_scratch(pieces, stages, devices)
    low = lambda *shape: jax.ShapeDtypeStruct(shape, jnp.bfloat16)
    full = lambda *shape: jax.ShapeDtypeStruct(shape, jnp.float32)
    any_ = pl.BlockSpec(memory_space=pl.ANY)
    sems = lambda *shape: pltpu.SemaphoreType.DMA(shape)
    lows = lambda *shape: pltpu.VMEM(shape, jnp.bfloat16)
    fulls = lambda *shape: pltpu.VMEM(shape, jnp.float32)
    scratch = [
        lows(depth, depth),
        lows(depth, hidden),
        lows(2, CHUNK, depth),
        lows(heads, rows, width),
        lows(rows, hidden),
        fulls(rows, hidden),
        lows(rows, hidden),
        fulls(rows, depth),
        fulls(rows, depth),
        fulls(rows, depth),
        lows(heads, rows, width),
    ]
    scratch += [lows(devices, block, part) for part in DOWN_PARTS]
    scratch += buffers
    scratch += [sems(2), sems(2), sems(2, 2, heads - 1), halver_sems]
    count = len(pieces)
    sizes = [0] * 17 + [2 * count] + [0] * 13 + [count, buffer_count] + [0] * 4
    outs = [
        low(rows, depth),
        full(rows, depth),
        low(rows, depth),
        low(rows, hidden),
        low(rows, depth),
        low(rows, depth),
        low(span, width),
    ]
    outs += left_over([piece for piece in pieces for _ in (0, 1)], [1], devices)
    outs += [full(SUB, depth), full(1, hidden)]
    return pl.pallas_call(
        unpack_refs(functools.partial(feed_kernel, stages), sizes),
        in_specs=[VMEM] * 7 + [any_] * 3,
        out_specs=[VMEM] * len(outs),
        out_shape=outs,
        scratch_shapes=scratch,
        compiler_params=pltpu.CompilerParams(
            collective_id=collective_id, has_side_effects=True, vmem_limit_bytes=63 * MIB
        ),
        name="feed",
    )(
        attended, tokens, out_grad, gain, bias, up_bias, down_bias, w_output, w_up, w_down
    )


def layer_norm(row_block, gain, bias):
    centre = jnp.mean(row_block, axis=-1, keepdims=True)
    centred = row_block - centre
    spread = jnp.mean(centred * centred, axis=-1, keepdims=True)
    return centred * lax.rsqrt(spread + epsilon) * gain + bias


def product(left, right):
    return jnp.dot(left, right, preferred_element_type=jnp.float32)


def product_left(left, right):
    return lax.dot_general(
        left, right, (((0,), (0,)), ((), ())), preferred_element_type=jnp.float32
    )


def product_right(left, right):
    return lax.dot_general(
        left, right, (((1,), (1,)), ((), ())), preferred_element_type=jnp.float32
    )


def per_device(
    tokens_in,
    seq_starts,
    block_sizes,
    norm1_gain,
    norm1_bias,
    w_query,
    w_key,
    w_value,
    w_output,
    ssm_rate,
    ssm_input,
    ssm_output,
    ssm_skip,
    norm2_gain,
    norm2_bias,
    w_up,
    up_bias,
    w_down,
    down_bias,
    out_grad,
):
    tok_rows = tokens_in.shape[0]
    pieces = lax.axis_size("tok")
    span = tok_rows * lax.axis_size("head")
    total_len = span * pieces

    rate = ssm_rate.T / total_len
    drive_in, read_out = ssm_input.T, ssm_output.T
    decay = jnp.exp(-rate)
    gain = jnp.sqrt(-jnp.expm1(-2.0 * rate))
    driving = gain * drive_in
    mix = read_out * driving
    skip = ssm_skip[None, :]
    hid, query_h, key_h, value_h, hidden_h, w_own, context, rims = front(
        seq_starts,
        tokens_in,
        norm1_gain[None, :],
        norm1_bias[None, :],
        rate,
        mix,
        skip,
        w_query,
        w_key,
        w_value,
        6,
    )
    attended, attended_fine, level = attend(seq_starts, block_sizes, query_h, key_h, value_h, context, rims)
    (
        layer_out,
        grad_middle,
        normed_low,
        grad_before_low,
        joined,
        grad_branch,
        grad_att,
        *down,
        vectors,
        grad_up_bias,
    ) = feed(
        attended,
        tokens_in,
        out_grad,
        norm2_gain[None, :],
        norm2_bias[None, :],
        up_bias[None, :],
        down_bias[None, :],
        w_output,
        w_up,
        w_down,
        7,
    )
    orders = halving_orders(bits_of(pieces * lax.axis_size("head")))
    come = [
        swapped(leave, orders[order][1]) for leave, order in zip(down[1::2], DOWN_ORDERS)
    ]

    back_query_h, key_rim, value_rim, near_rim, back_key_h, back_value_h, back_context = attend_back(
        seq_starts, block_sizes, query_h, key_h, value_h, context, rims, attended_fine, grad_att, level
    )
    (
        back_key_h,
        back_value_h,
        back_feed_h,
        sums,
        lag_sums,
        skip_sum,
        out_w_down,
        up,
        apart,
    ) = recurrence_back(
        seq_starts,
        back_context,
        hidden_h,
        rate,
        mix,
        skip,
        [back_key_h, back_value_h],
        [key_rim, value_rim, near_rim],
        [normed_low, joined],
        [grad_before_low, grad_branch],
        (down[::2], come),
        2,
    )
    input_grad, out_w_heads, summed, packed, up = head_backward(
        back_query_h,
        back_key_h,
        back_value_h,
        back_feed_h,
        hid,
        w_own,
        tokens_in,
        norm1_gain[None, :],
        grad_middle,
        sums,
        lag_sums,
        skip_sum,
        vectors,
        grad_up_bias,
        up,
        4,
    )
    heads, head = lax.axis_size("head"), lax.axis_index("head")
    part = norm1_gain.shape[0] // pieces
    more = up_bias.shape[0] // norm1_gain.shape[0]
    short = lax.dynamic_slice_in_dim(packed[:5], head * (part // heads), part // heads, 1)
    out_up_bias = lax.dynamic_slice_in_dim(
        packed[5 : 5 + more, :part].reshape(-1), head * (more * part // heads), more * part // heads
    )
    out_w_up, out_w_output = up if apart is None else apart
    sums, lag_sums, skip_sum = summed[:NS], summed[NS : 2 * NS], summed[2 * NS]
    grad_ssm_output = (driving * sums).T
    grad_driving = read_out * sums
    grad_ssm_input = (gain * grad_driving).T
    grad_ssm_rate = (
        grad_driving * drive_in * jnp.exp(-2.0 * rate) / gain - mix * lag_sums * decay
    ).T / total_len

    return (
        layer_out,
        input_grad,
        short[0],
        short[1],
        out_w_heads[0],
        out_w_heads[1],
        out_w_heads[2],
        out_w_output,
        grad_ssm_rate,
        grad_ssm_input,
        grad_ssm_output,
        skip_sum,
        short[2],
        short[3],
        out_w_up,
        out_up_bias,
        out_w_down,
        short[4],
    )


def solution(mesh):
    return jax.shard_map(
        per_device,
        mesh=mesh,
        in_specs=(
            P(("tok", "head"), None),
            P(),
            P(),
            P(),
            P(),
            P(),
            P(),
            P(),
            P(),
            P("head", None),
            P("head", None),
            P("head", None),
            P("head"),
            P(),
            P(),
            P(),
            P(),
            P(),
            P(),
            P(("tok", "head"), None),
        ),
        out_specs=(
            P(("tok", "head"), None),
            P(("tok", "head"), None),
            P(("tok", "head")),
            P(("tok", "head")),
            P(("tok", "head"), None),
            P(("tok", "head"), None),
            P(("tok", "head"), None),
            P(("tok", "head"), None),
            P("head", None),
            P("head", None),
            P("head", None),
            P("head"),
            P(("tok", "head")),
            P(("tok", "head")),
            P(("tok", "head"), None),
            P(("tok", "head")),
            P(("tok", "head"), None),
            P(("tok", "head")),
        ),
        check_vma=False,
    )
```

profile of v0, /device:TPU:0, one launch (start us, length us, event | category | flops | bytes accessed | tf_op | source)
XLA Modules:
  0.0 285.8 jit_solution(2463753076745878978)
XLA Ops:
  0.7 1.3 multiply_bitcast_fusion.1.rate.refs_3_
  2.0 1.4 bitcast_multiply_fusion.5.mix.refs_4_
  3.4 52.4 %front.1 = (bf16[1536,1024]{1,0:T(8,128)(2,1)}, bf16[1536,256]{1,0:T(8,128)(2,1)}, bf16[1536,256]{1,0:T(8,128)(2,1)}, bf16[1536,256]{1,0:T(8,128)(2,1)}, bf16[15...) custom-call(s32[2]{0:T(128)} %refs_0_.1, ...), custom_call_target="tpu_custom_call" | custom-call | tf_op jit(solution)/shard_map/front/pallas_call | solution.py:1220
  55.8 15.3 %attend.1 = (bf16[1536,256]{1,0:T(8,128)(2,1)}, f32[1536,256]{1,0:T(8,128)}, f32[2,6,1,256]{3,2,1,0:T(1,128)}) custom-call(s32[2]{0:T(128)} %refs_0_.1, s32[2]{0:T(128)} %sizes.3, bf16[1536,256]{1,0:T(8,128)(2,1)} %get-tuple-element.71.query, bf16[1536,256]{1,0:T(8,128)(2,1)} %get-tuple-element.72.key_own, bf16[1536,256]{1,0:T(8,128)(2,1)} %get-tuple-element.73.value_own, ...), custom_call_target="tpu_custom_call" | custom-call | tf_op jit(solution)/shard_map/attend/pallas_call | solution.py:310
  71.1 50.1 %feed.1 = (bf16[384,1024]{1,0:T(8,128)(2,1)}, f32[384,1024]{1,0:T(8,128)}, bf16[384,1024]{1,0:T(8,128)(2,1)}, bf16[384,4096]{1,0:T(8,128)(2,1)}, bf16[384,1024]{...) custom-call(bf16[1536,256]{1,0:T(8,128)(2,1)} %get-tuple-element.78., ...), custom_call_target="tpu_custom_call" | custom-call | tf_op jit(solution)/shard_map/feed/pallas_call | solution.py:1819
  121.7 1.0 collective-permute-start.2
  122.7 1.2 collective-permute-start
  124.0 18.8 %attend_back.1 = (bf16[1536,256]{1,0:T(8,128)(2,1)}, bf16[512,256]{1,0:T(8,128)(2,1)}, bf16[512,256]{1,0:T(8,128)(2,1)}, bf16[640,256]{1,0:T(8,128)(2,1)}, f32[1...) custom-call(s32[2]{0:T(128)} %refs_0_.1, s32[2]{0:T(128)} %sizes.3, ...), custom_call_target="tpu_custom_call" | custom-call | tf_op jit(solution)/shard_map/attend_back/pallas_call | solution.py:338
  142.9 0.7 copy-done.4
  144.2 66.1 %recurrence_back.1 = (bf16[1536,256]{1,0:T(8,128)(2,1)}, bf16[1536,256]{1,0:T(8,128)(2,1)}, bf16[1536,256]{1,0:T(8,128)(2,1)}, f32[16,256]{1,0:T(8,128)}, f32[16...) custom-call(s32[2]{0:T(128)} %refs_0_.1, ...), custom_call_target="tpu_custom_call" | custom-call | tf_op jit(solution)/shard_map/recurrence_back/pallas_call | solution.py:1530
  210.3 63.4 %head_backward.1 = (f32[384,1024]{1,0:T(8,128)}, f32[32,1024]{1,0:T(8,128)}, f32[32,1024]{1,0:T(8,128)}, f32[32,1024]{1,0:T(8,128)}, f32[40,256]{1,0:T(8,128)}, ...) custom-call(bf16[1536,256]{1,0:T(8,128)(2,1)} %get-tuple-element.83.refs_0_, ...), custom_call_target="tpu_custom_call" | custom-call | tf_op jit(solution)/shard_map/head_backward/pallas_call | solution.py:919
  273.7 0.8 slice.30
  274.5 0.7 slice_bitcast_fusion
  275.2 1.4 multiply_bitcast_fusion
  276.6 1.3 slice.35
  278.4 0.6 dynamic_slice.7
  279.0 0.9 copy.46
  279.9 1.1 copy.47
  281.1 0.7 copy.48
  281.8 0.7 copy.49
  282.4 0.7 copy.50
  283.1 0.7 copy.51
  283.7 0.8 copy.52
  284.5 0.8 copy.53
  (33 shorter events, 1.8 us)
Async XLA Ops:
  121.2 21.6 %collective-permute-start.1 = (bf16[8,128,384]{2,1,0:T(8,128)(2,1)}, bf16[8,128,384]{2,1,0:T(8,128)(2,1)S(1)}, u32[]{:S(2)}, u32[]{:S(2)}) collective-permute-start(bf16[8,128,384]{2,1,0:T(8,128)(2,1)} %get-tuple-element.99), channel_id=1, source_target_pairs={{0,4},{4,0},{8,12},{12,8},{16,20},{20,16},{24,28},{28,24},{1,5},{5... | collective-permute-start | bytes 2359304 | tf_op jit(solution)/shard_map/ppermute | solution.py:557
  121.7 21.1 %collective-permute-start.2 = (bf16[8,128,384]{2,1,0:T(8,128)(2,1)}, bf16[8,128,384]{2,1,0:T(8,128)(2,1)S(1)}, u32[]{:S(2)}, u32[]{:S(2)}) collective-permute-start(bf16[8,128,384]{2,1,0:T(8,128)(2,1)} %get-tuple-element.100), channel_id=1, source_target_pairs={{0,8},{4,12},{8,0},{12,4},{16,24},{20,28},{24,16},{28,20},{1,9},{5... | collective-permute-start | bytes 2359304 | tf_op jit(solution)/shard_map/ppermute | solution.py:557
  122.7 20.1 %collective-permute-start = (bf16[8,128,256]{2,1,0:T(8,128)(2,1)}, bf16[8,128,256]{2,1,0:T(8,128)(2,1)S(1)}, u32[]{:S(2)}, u32[]{:S(2)}) collective-permute-start(bf16[8,128,256]{2,1,0:T(8,128)(2,1)} %get-tuple-element.98), channel_id=1, source_target_pairs={{0,2},{1,3},{2,0},{3,1},{4,6},{5,7},{6,4},{7,5},{8,10},{9,11},{10,... | collective-permute-start | bytes 1572872 | tf_op jit(solution)/shard_map/ppermute | solution.py:557
  142.8 0.8 copy-start.4
  142.8 1.0 copy-start.1
  142.8 1.4 copy-start.2
  210.3 64.9 %copy-start.7 = (f32[256,16]{0,1:T(8,128)S(1)}, f32[256,16]{0,1:T(8,128)}, u32[]{:S(2)}) copy-start(f32[256,16]{0,1:T(8,128)} %param.29) | copy-start | bytes 49156
  210.3 64.9 %copy-start.12 = (f32[256,16]{0,1:T(8,128)S(1)}, f32[256,16]{0,1:T(8,128)}, u32[]{:S(2)}) copy-start(f32[256,16]{0,1:T(8,128)} %param.31) | copy-start | bytes 49156
  210.3 64.9 %copy-start.13 = (f32[256,16]{0,1:T(8,128)S(1)}, f32[256,16]{0,1:T(8,128)}, u32[]{:S(2)}) copy-start(f32[256,16]{0,1:T(8,128)} %param.30) | copy-start | bytes 49156
  210.3 68.7 %copy-start.3 = (bf16[384,1024]{1,0:T(8,128)(2,1)S(1)}, bf16[384,1024]{1,0:T(8,128)(2,1)}, u32[]{:S(2)}) copy-start(bf16[384,1024]{1,0:T(8,128)(2,1)} %get-tuple-element.150) | copy-start | bytes 2359300
  273.7 6.2 %copy-start = (f32[384,1024]{1,0:T(8,128)S(1)}, f32[384,1024]{1,0:T(8,128)}, u32[]{:S(2)}) copy-start(f32[384,1024]{1,0:T(8,128)} %get-tuple-element.151) | copy-start | bytes 4718596
  279.9 1.2 copy-start.11
  279.9 1.8 copy-start.10
  279.9 2.5 copy-start.9
  279.9 3.1 %copy-start.8 = (f32[32,1024]{1,0:T(8,128)S(1)}, f32[32,1024]{1,0:T(8,128)}, u32[]{:S(2)}) copy-start(f32[32,1024]{1,0:T(8,128)} %get-tuple-element.157) | copy-start | bytes 393220
  279.9 3.8 %copy-start.6 = (f32[32,4096]{1,0:T(8,128)S(1)}, f32[32,4096]{1,0:T(8,128)}, u32[]{:S(2)}) copy-start(f32[32,4096]{1,0:T(8,128)} %get-tuple-element.164) | copy-start | bytes 1572868
  281.1 3.4 %copy-start.5 = (f32[128,1024]{1,0:T(8,128)S(1)}, f32[128,1024]{1,0:T(8,128)}, u32[]{:S(2)}) copy-start(f32[128,1024]{1,0:T(8,128)} %get-tuple-element.166) | copy-start | bytes 1572868
where the time goes:
time: 291 us; the launch traced here: 286 us
  Pallas kernels  266 us (91%)
  local copies, waits for them, and re-layouts  11.6 us (4%)
  other arithmetic  4.09 us (1%)
    pallas_call x1, Pallas kernels, recurrence_back(): pl.pallas_call(unpack_refs(functools.partial(recurrence_back_kernel, stag...  66.1 us
    pallas_call x1, Pallas kernels, head_backward(): pl.pallas_call(unpack_refs(functools.partial(head_backward_kernel, stages...  63.4 us
    pallas_call x1, Pallas kernels, front(): pl.pallas_call(front_kernel, in_specs=[SCALARS] + [VMEM] * 6 + [pl.BlockS...  52.4 us
    pallas_call x1, Pallas kernels, feed(): pl.pallas_call(unpack_refs(functools.partial(feed_kernel, stages), sizes)...  50.1 us
    pallas_call x1, Pallas kernels, attend_back(): pl.pallas_call(attend_back_kernel, in_specs=[SCALARS] * 2 + [VMEM] * 10,...  18.8 us
    pallas_call x1, Pallas kernels, attend(): pl.pallas_call(attend_kernel, in_specs=[SCALARS] * 2 + [VMEM] * 7, out_sp...  15.3 us
    unnamed x36, local copies, waits for them, and re-layouts  7.63 us
  transfers between devices with their start and end apart: 3, of which 0 were waited for; matrix products, arithmetic and copies ran while one was open for 0% of the time, Pallas kernels for 7%

commit v1 on v0

--- a/solution.py
+++ b/solution.py
@@ -1437,10 +1437,9 @@
                 return tuple(adjoint) + tuple(lag) + tuple(direct) + tuple(late_sum)
 
             if group == 0 and base > 0:
-                down.advance(0)
                 down.advance(1)
                 down.advance(2)
-            if group == 1 and base == 0:
+            if group == 1:
                 down.advance(0)
             first = tuple(ends[base + n, :, lanes] for n in range(HALF)) + tuple(
                 lags[base + n, :, lanes] for n in range(HALF)

time: 291 us -> 291 us (level)
  no operation moved by 1% of the time
where the time goes in v1:
time: 291 us; the launch traced here: 286 us
  Pallas kernels  265 us (91%)
  local copies, waits for them, and re-layouts  11.6 us (4%)
  other arithmetic  4.09 us (1%)
  starting transfers between devices  3.36 us (1%)
    pallas_call x1, Pallas kernels, recurrence_back(): pl.pallas_call(unpack_refs(functools.partial(recurrence_back_kernel, stag...  64.6 us
    pallas_call x1, Pallas kernels, head_backward(): pl.pallas_call(unpack_refs(functools.partial(head_backward_kernel, stages...  64.2 us
    pallas_call x1, Pallas kernels, front(): pl.pallas_call(front_kernel, in_specs=[SCALARS] + [VMEM] * 6 + [pl.BlockS...  52.4 us
    pallas_call x1, Pallas kernels, feed(): pl.pallas_call(unpack_refs(functools.partial(feed_kernel, stages), sizes)...  48.8 us
    pallas_call x1, Pallas kernels, attend_back(): pl.pallas_call(attend_back_kernel, in_specs=[SCALARS] * 2 + [VMEM] * 10,...  19.5 us
    pallas_call x1, Pallas kernels, attend(): pl.pallas_call(attend_kernel, in_specs=[SCALARS] * 2 + [VMEM] * 7, out_sp...  16.1 us
    unnamed x36, local copies, waits for them, and re-layouts  7.63 us
  transfers between devices with their start and end apart: 3, of which 0 were waited for; matrix products, arithmetic and copies ran while one was open for 0% of the time, Pallas kernels for 7%

profile of v1, /device:TPU:0, one launch (start us, length us, event | category | flops | bytes accessed | tf_op | source)
XLA Modules:
  0.0 285.8 jit_solution(10069550684635978771)
XLA Ops:
  0.7 1.3 multiply_bitcast_fusion.1.rate.refs_3_
  2.0 1.4 bitcast_multiply_fusion.5.mix.refs_4_
  3.4 52.4 %front.1 = (bf16[1536,1024]{1,0:T(8,128)(2,1)}, bf16[1536,256]{1,0:T(8,128)(2,1)}, bf16[1536,256]{1,0:T(8,128)(2,1)}, bf16[1536,256]{1,0:T(8,128)(2,1)}, bf16[15...) custom-call(s32[2]{0:T(128)} %refs_0_.1, ...), custom_call_target="tpu_custom_call" | custom-call | tf_op jit(solution)/shard_map/front/pallas_call | solution.py:1220
  55.8 16.1 %attend.1 = (bf16[1536,256]{1,0:T(8,128)(2,1)}, f32[1536,256]{1,0:T(8,128)}, f32[2,6,1,256]{3,2,1,0:T(1,128)}) custom-call(s32[2]{0:T(128)} %refs_0_.1, s32[2]{0:T(128)} %sizes.3, bf16[1536,256]{1,0:T(8,128)(2,1)} %get-tuple-element.71.query, bf16[1536,256]{1,0:T(8,128)(2,1)} %get-tuple-element.72.key_own, bf16[1536,256]{1,0:T(8,128)(2,1)} %get-tuple-element.73.value_own, ...), custom_call_target="tpu_custom_call" | custom-call | tf_op jit(solution)/shard_map/attend/pallas_call | solution.py:310
  71.8 48.8 %feed.1 = (bf16[384,1024]{1,0:T(8,128)(2,1)}, f32[384,1024]{1,0:T(8,128)}, bf16[384,1024]{1,0:T(8,128)(2,1)}, bf16[384,4096]{1,0:T(8,128)(2,1)}, bf16[384,1024]{...) custom-call(bf16[1536,256]{1,0:T(8,128)(2,1)} %get-tuple-element.78., ...), custom_call_target="tpu_custom_call" | custom-call | tf_op jit(solution)/shard_map/feed/pallas_call | solution.py:1818
  120.6 0.6 collective-permute-start.1
  121.3 1.4 collective-permute-start.2
  122.7 1.3 collective-permute-start
  124.0 19.5 %attend_back.1 = (bf16[1536,256]{1,0:T(8,128)(2,1)}, bf16[512,256]{1,0:T(8,128)(2,1)}, bf16[512,256]{1,0:T(8,128)(2,1)}, bf16[640,256]{1,0:T(8,128)(2,1)}, f32[1...) custom-call(s32[2]{0:T(128)} %refs_0_.1, s32[2]{0:T(128)} %sizes.3, ...), custom_call_target="tpu_custom_call" | custom-call | tf_op jit(solution)/shard_map/attend_back/pallas_call | solution.py:338
  143.6 0.7 copy-done.4
  144.9 64.6 %recurrence_back.1 = (bf16[1536,256]{1,0:T(8,128)(2,1)}, bf16[1536,256]{1,0:T(8,128)(2,1)}, bf16[1536,256]{1,0:T(8,128)(2,1)}, f32[16,256]{1,0:T(8,128)}, f32[16...) custom-call(s32[2]{0:T(128)} %refs_0_.1, ...), custom_call_target="tpu_custom_call" | custom-call | tf_op jit(solution)/shard_map/recurrence_back/pallas_call | solution.py:1529
  209.5 64.2 %head_backward.1 = (f32[384,1024]{1,0:T(8,128)}, f32[32,1024]{1,0:T(8,128)}, f32[32,1024]{1,0:T(8,128)}, f32[32,1024]{1,0:T(8,128)}, f32[40,256]{1,0:T(8,128)}, ...) custom-call(bf16[1536,256]{1,0:T(8,128)(2,1)} %get-tuple-element.83.refs_0_, ...), custom_call_target="tpu_custom_call" | custom-call | tf_op jit(solution)/shard_map/head_backward/pallas_call | solution.py:919
  273.7 0.8 slice.30
  274.5 0.7 slice_bitcast_fusion
  275.2 1.4 multiply_bitcast_fusion
  276.6 1.3 slice.35
  279.0 0.9 copy.46
  279.9 1.1 copy.47
  281.1 0.7 copy.48
  281.8 0.7 copy.49
  282.4 0.7 copy.50
  283.1 0.7 copy.51
  283.7 0.8 copy.52
  284.5 0.8 copy.53
  (33 shorter events, 1.9 us)
Async XLA Ops:
  120.6 22.9 %collective-permute-start.1 = (bf16[8,128,384]{2,1,0:T(8,128)(2,1)}, bf16[8,128,384]{2,1,0:T(8,128)(2,1)S(1)}, u32[]{:S(2)}, u32[]{:S(2)}) collective-permute-start(bf16[8,128,384]{2,1,0:T(8,128)(2,1)} %get-tuple-element.99), channel_id=1, source_target_pairs={{0,4},{4,0},{8,12},{12,8},{16,20},{20,16},{24,28},{28,24},{1,5},{5... | collective-permute-start | bytes 2359304 | tf_op jit(solution)/shard_map/ppermute | solution.py:557
  121.3 22.2 %collective-permute-start.2 = (bf16[8,128,384]{2,1,0:T(8,128)(2,1)}, bf16[8,128,384]{2,1,0:T(8,128)(2,1)S(1)}, u32[]{:S(2)}, u32[]{:S(2)}) collective-permute-start(bf16[8,128,384]{2,1,0:T(8,128)(2,1)} %get-tuple-element.100), channel_id=1, source_target_pairs={{0,8},{4,12},{8,0},{12,4},{16,24},{20,28},{24,16},{28,20},{1,9},{5... | collective-permute-start | bytes 2359304 | tf_op jit(solution)/shard_map/ppermute | solution.py:557
  122.7 20.8 %collective-permute-start = (bf16[8,128,256]{2,1,0:T(8,128)(2,1)}, bf16[8,128,256]{2,1,0:T(8,128)(2,1)S(1)}, u32[]{:S(2)}, u32[]{:S(2)}) collective-permute-start(bf16[8,128,256]{2,1,0:T(8,128)(2,1)} %get-tuple-element.98), channel_id=1, source_target_pairs={{0,2},{1,3},{2,0},{3,1},{4,6},{5,7},{6,4},{7,5},{8,10},{9,11},{10,... | collective-permute-start | bytes 1572872 | tf_op jit(solution)/shard_map/ppermute | solution.py:557
  143.5 0.8 copy-start.4
  143.5 1.0 copy-start.1
  143.5 1.4 copy-start.2
  209.5 65.7 %copy-start.7 = (f32[256,16]{0,1:T(8,128)S(1)}, f32[256,16]{0,1:T(8,128)}, u32[]{:S(2)}) copy-start(f32[256,16]{0,1:T(8,128)} %param.29) | copy-start | bytes 49156
  209.5 65.7 %copy-start.12 = (f32[256,16]{0,1:T(8,128)S(1)}, f32[256,16]{0,1:T(8,128)}, u32[]{:S(2)}) copy-start(f32[256,16]{0,1:T(8,128)} %param.31) | copy-start | bytes 49156
  209.5 65.7 %copy-start.13 = (f32[256,16]{0,1:T(8,128)S(1)}, f32[256,16]{0,1:T(8,128)}, u32[]{:S(2)}) copy-start(f32[256,16]{0,1:T(8,128)} %param.30) | copy-start | bytes 49156
  209.5 69.5 %copy-start.3 = (bf16[384,1024]{1,0:T(8,128)(2,1)S(1)}, bf16[384,1024]{1,0:T(8,128)(2,1)}, u32[]{:S(2)}) copy-start(bf16[384,1024]{1,0:T(8,128)(2,1)} %get-tuple-element.150) | copy-start | bytes 2359300
  273.7 6.2 %copy-start = (f32[384,1024]{1,0:T(8,128)S(1)}, f32[384,1024]{1,0:T(8,128)}, u32[]{:S(2)}) copy-start(f32[384,1024]{1,0:T(8,128)} %get-tuple-element.151) | copy-start | bytes 4718596
  279.9 1.2 copy-start.11
  279.9 1.8 copy-start.10
  279.9 2.5 copy-start.9
  279.9 3.1 %copy-start.8 = (f32[32,1024]{1,0:T(8,128)S(1)}, f32[32,1024]{1,0:T(8,128)}, u32[]{:S(2)}) copy-start(f32[32,1024]{1,0:T(8,128)} %get-tuple-element.157) | copy-start | bytes 393220
  279.9 3.8 %copy-start.6 = (f32[32,4096]{1,0:T(8,128)S(1)}, f32[32,4096]{1,0:T(8,128)}, u32[]{:S(2)}) copy-start(f32[32,4096]{1,0:T(8,128)} %get-tuple-element.164) | copy-start | bytes 1572868
  281.1 3.4 %copy-start.5 = (f32[128,1024]{1,0:T(8,128)S(1)}, f32[128,1024]{1,0:T(8,128)}, u32[]{:S(2)}) copy-start(f32[128,1024]{1,0:T(8,128)} %get-tuple-element.166) | copy-start | bytes 1572868
